TPU v7x, 128 devices: a whole 4x4x4 slice. The times are simulated.
128 devices in a mesh: dp: 32 (over x, y, z_hi), tensor: 4 (over z_lo, core).
Axes of the slice: x: 4, y: 4, z: 4 (z_hi: 2, z_lo: 2; z = z_hi * 2 + z_lo), core: 2. Of those that a mesh axis runs over, the one named last changes fastest.
Arguments:
- input_frames: bfloat16 [32768, 768], P(('dp', 'tensor')), may hold values from -6 to 6
- cotangent: bfloat16 [32768, 768], P(('dp', 'tensor')), may hold values from -24 to 24
- attention_in: bfloat16 [2, 3, 768, 768], P(None, None, 'dp', 'tensor'), may hold values from -0.21875 to 0.21875
- attention_bias: bfloat16 [2, 2, 768], P(None, None, ('tensor', 'dp')), may hold values from -3 to 3
- attention_out: bfloat16 [2, 768, 768], P(None, 'tensor', 'dp'), may hold values from -0.4375 to 0.4375
- up_weight: bfloat16 [2, 768, 3072], P(None, 'dp', 'tensor'), may hold values from -0.21875 to 0.21875
- up_bias: bfloat16 [2, 3072], P(None, ('tensor', 'dp')), may hold values from -3 to 3
- down_weight: bfloat16 [2, 3072, 768], P(None, 'tensor', 'dp'), may hold values from -0.109375 to 0.109375
- norm_gains: float32 [2, 2, 768], P(None, None, ('dp', 'tensor')), may hold values from 0.1 to 1.9
- row_shifts: float32 [2, 4, 768], P(None, None, ('dp', 'tensor')), may hold values from -2 to 2
Outputs:
- output_frames: float32 [32768, 768], P(('dp', 'tensor'))
- grad_frames: float32 [32768, 768], P(('dp', 'tensor'))
- grad_attention_in: float32 [2, 3, 768, 768], P(None, None, 'dp', 'tensor')
- grad_attention_bias: float32 [2, 2, 768], P(None, None, ('tensor', 'dp'))
- grad_attention_out: float32 [2, 768, 768], P(None, 'tensor', 'dp')
- grad_up_weight: float32 [2, 768, 3072], P(None, 'dp', 'tensor')
- grad_up_bias: float32 [2, 3072], P(None, ('tensor', 'dp'))
- grad_down_weight: float32 [2, 3072, 768], P(None, 'tensor', 'dp')
- grad_norm_gains: float32 [2, 2, 768], P(None, None, ('dp', 'tensor'))
- grad_row_shifts: float32 [2, 4, 768], P(None, None, ('dp', 'tensor'))
All inputs are finite; a program needn't handle non-finite values.
Results may differ from a plain program's by a relative error of at most 0.01.
Values may be sent and summed in bfloat16 or wider, within the bound.
No kernel may reach another device: no remote copies, remote signals or barrier semaphores. Data moves between devices by JAX's collectives and lax.ppermute only.
A program may use at most 192 MiB of HBM per device.

v0:
```python
import jax
import jax.numpy as jnp
from jax import lax
from jax.sharding import PartitionSpec as P

HEAD_DIM = 64
FRAMES = 1024


norm_eps = 1e-05
score_scale = 0.125
root_half = 0.7071067811865476
inv_root_two_pi = 0.3989422804014327


def norm_forward(stream, gain_row, shift_row):
    row_mean = jnp.mean(stream, axis=-1, keepdims=True)
    centred = stream - row_mean
    variance = jnp.mean(centred * centred, axis=-1, keepdims=True)
    inverse = lax.rsqrt(variance + norm_eps)
    scaled = centred * inverse
    return (scaled * gain_row + shift_row, scaled, inverse)


def norm_backward(grad_output, scaled, inverse, gain_row):
    grad_scaled = grad_output * gain_row
    mean_grad = jnp.mean(grad_scaled, axis=-1, keepdims=True)
    mean_cross = jnp.mean(grad_scaled * scaled, axis=-1, keepdims=True)
    grad_input = inverse * (grad_scaled - mean_grad - scaled * mean_cross)
    return (grad_input, jnp.sum(grad_output * scaled, axis=0), jnp.sum(grad_output, axis=0))


def gelu_slope(hidden):
    normal_cdf = 0.5 * (1.0 + lax.erf(hidden * root_half))
    return normal_cdf + hidden * jnp.exp(-0.5 * hidden * hidden) * inv_root_two_pi


def matmul(left_side, right_side):
    return jnp.dot(left_side, right_side, preferred_element_type=jnp.float32)


def inner_rows(left_side, right_side):
    return lax.dot_general(
        left_side, right_side, (((0,), (0,)), ((), ())), preferred_element_type=jnp.float32
    )


def times_transpose(left_side, right_side):
    return lax.dot_general(
        left_side, right_side, (((1,), (1,)), ((), ())), preferred_element_type=jnp.float32
    )


def gather_rows(values):
    return lax.all_gather(values, "tensor", axis=0, tiled=True)


def scatter_rows(values):
    return lax.psum_scatter(values, "tensor", scatter_dimension=0, tiled=True)


def gather_grads(values):
    return lax.all_gather(values, "tensor", axis=0, tiled=True)


def scatter_grads(values):
    return lax.psum_scatter(values, "tensor", scatter_dimension=0, tiled=True)


def reduce_weights(grad_tuple):
    return (
        lax.psum_scatter(grad_tuple[0], "dp", scatter_dimension=2, tiled=True),
        lax.psum_scatter(grad_tuple[1], "dp", scatter_dimension=2, tiled=True),
        lax.psum_scatter(grad_tuple[2], "dp", scatter_dimension=2, tiled=True),
        lax.psum_scatter(grad_tuple[3], "dp", scatter_dimension=1, tiled=True),
        lax.psum_scatter(grad_tuple[4], "dp", scatter_dimension=1, tiled=True),
        lax.psum_scatter(grad_tuple[5], "dp", scatter_dimension=2, tiled=True),
    )


def attend_clip(queries, key_rows, values, block_rows):
    mixtures = []
    log_sums = []
    for offset in range(0, queries.shape[0], block_rows):
        query_part = queries[offset : offset + block_rows]
        scores = (
            jnp.einsum("qhd,khd->hqk", query_part, key_rows, preferred_element_type=jnp.float32)
            * score_scale
        )
        row_max = jnp.max(scores, axis=-1, keepdims=True)
        shifted_exp = jnp.exp(scores - row_max)
        exp_total = jnp.sum(shifted_exp, axis=-1, keepdims=True)
        attention = (shifted_exp / exp_total).astype(jnp.bfloat16)
        mixture = jnp.einsum("hqk,khd->qhd", attention, values, preferred_element_type=jnp.float32)
        mixtures.append(mixture.astype(jnp.bfloat16))
        log_sums.append(row_max + jnp.log(exp_total))
    return (jnp.concatenate(mixtures, axis=0), jnp.concatenate(log_sums, axis=1))


def attend_back(queries, key_rows, values, log_sum, grad_mixture, block_rows):
    grad_keys = jnp.zeros(key_rows.shape, jnp.float32)
    grad_values = jnp.zeros(values.shape, jnp.float32)
    grad_query_parts = []
    for offset in range(0, queries.shape[0], block_rows):
        query_part = queries[offset : offset + block_rows]
        grad_part = grad_mixture[offset : offset + block_rows]
        scores = (
            jnp.einsum("qhd,khd->hqk", query_part, key_rows, preferred_element_type=jnp.float32)
            * score_scale
        )
        attention = jnp.exp(scores - log_sum[:, offset : offset + block_rows])
        grad_attention = jnp.einsum(
            "qhd,khd->hqk", grad_part, values, preferred_element_type=jnp.float32
        )
        row_delta = jnp.sum(attention * grad_attention, axis=-1, keepdims=True)
        grad_scores = (attention * (grad_attention - row_delta)).astype(jnp.bfloat16)
        grad_query_parts.append(
            jnp.einsum("hqk,khd->qhd", grad_scores, key_rows, preferred_element_type=jnp.float32)
            * score_scale
        )
        grad_keys = (
            grad_keys
            + jnp.einsum(
                "hqk,qhd->khd", grad_scores, query_part, preferred_element_type=jnp.float32
            )
            * score_scale
        )
        grad_values = grad_values + jnp.einsum(
            "hqk,qhd->khd",
            attention.astype(jnp.bfloat16),
            grad_part,
            preferred_element_type=jnp.float32,
        )
    grad_queries = jnp.concatenate(grad_query_parts, axis=0)
    return (
        grad_queries.astype(jnp.bfloat16),
        grad_keys.astype(jnp.bfloat16),
        grad_values.astype(jnp.bfloat16),
    )


def per_device(
    input_frames,
    cotangent,
    attention_in,
    attention_bias,
    attention_out,
    up_weight,
    up_bias,
    down_weight,
    norm_gains,
    row_shifts,
):
    layers = attention_in.shape[0]
    frames = FRAMES
    head_dim = HEAD_DIM
    block_rows = 512
    full_gains, full_shifts = (
        lax.all_gather(norm_gains, ("dp", "tensor"), axis=2, tiled=True),
        lax.all_gather(row_shifts, ("dp", "tensor"), axis=2, tiled=True),
    )

    def fetch(layer_index):
        pieces = (
            lax.all_gather(attention_in[layer_index : layer_index + 1], "dp", axis=2, tiled=True),
            lax.all_gather(attention_bias[layer_index : layer_index + 1], "dp", axis=2, tiled=True),
            lax.all_gather(attention_out[layer_index : layer_index + 1], "dp", axis=2, tiled=True),
            lax.all_gather(up_weight[layer_index : layer_index + 1], "dp", axis=1, tiled=True),
            lax.all_gather(up_bias[layer_index : layer_index + 1], "dp", axis=1, tiled=True),
            lax.all_gather(down_weight[layer_index : layer_index + 1], "dp", axis=2, tiled=True),
        )
        return tuple((piece[0] for piece in pieces))

    stream = input_frames.astype(jnp.float32)
    stored = []
    fetched = []
    for layer_index in range(layers):
        weights = fetch(layer_index)
        fetched.append(weights)
        in_full, in_bias_full, out_full, up_full, up_bias_full, down_full = weights
        normed, scaled_one, inverse_one = norm_forward(
            stream, full_gains[layer_index, 0], full_shifts[layer_index, 0]
        )
        normed_all = gather_rows(normed.astype(jnp.bfloat16))
        total_rows = normed_all.shape[0]
        clip_count = total_rows // frames
        queries = (matmul(normed_all, in_full[0]) + in_bias_full[0].astype(jnp.float32)).astype(
            jnp.bfloat16
        )
        key_rows = matmul(normed_all, in_full[1]).astype(jnp.bfloat16)
        values = (matmul(normed_all, in_full[2]) + in_bias_full[1].astype(jnp.float32)).astype(
            jnp.bfloat16
        )
        local_heads = queries.shape[1] // head_dim
        head_shape = (clip_count, frames, local_heads, head_dim)
        queries = queries.reshape(head_shape)
        key_rows = key_rows.reshape(head_shape)
        values = values.reshape(head_shape)
        mixture, log_sum = lax.map(
            lambda operands: attend_clip(operands[0], operands[1], operands[2], block_rows),
            (queries, key_rows, values),
        )
        mixture = mixture.reshape(total_rows, -1)
        middle = stream + scatter_rows(matmul(mixture, out_full)) + full_shifts[layer_index, 1]
        lifted, scaled_two, inverse_two = norm_forward(
            middle, full_gains[layer_index, 1], full_shifts[layer_index, 2]
        )
        lifted_all = gather_rows(lifted.astype(jnp.bfloat16))
        hidden = matmul(lifted_all, up_full) + up_bias_full.astype(jnp.float32)
        active = jax.nn.gelu(hidden, approximate=False).astype(jnp.bfloat16)
        stream = middle + scatter_rows(matmul(active, down_full)) + full_shifts[layer_index, 3]
        stored.append(
            (
                normed_all,
                scaled_one,
                inverse_one,
                queries,
                key_rows,
                values,
                log_sum,
                mixture,
                scaled_two,
                inverse_two,
                lifted_all,
                hidden,
                active,
            )
        )
    grad_stream = cotangent.astype(jnp.float32)
    weight_grad_list = [None] * layers
    gain_grad_list = [None] * layers
    shift_grad_list = [None] * layers
    for layer_index in reversed(range(layers)):
        weights = fetch(layer_index)
        in_full, in_bias_full, out_full, up_full, up_bias_full, down_full = weights
        (
            normed_all,
            scaled_one,
            inverse_one,
            queries,
            key_rows,
            values,
            log_sum,
            mixture,
            scaled_two,
            inverse_two,
            lifted_all,
            hidden,
            active,
        ) = stored[layer_index]
        total_rows = normed_all.shape[0]
        head_shape = queries.shape
        grad_down_shift = jnp.sum(grad_stream, axis=0)
        branch_grad = gather_grads(grad_stream.astype(jnp.bfloat16))
        grad_down = inner_rows(active, branch_grad)
        grad_active = times_transpose(branch_grad, down_full)
        grad_hidden = (grad_active * gelu_slope(hidden)).astype(jnp.bfloat16)
        grad_up_bias = jnp.sum(grad_hidden.astype(jnp.float32), axis=0)
        grad_up = inner_rows(lifted_all, grad_hidden)
        grad_lifted = scatter_grads(times_transpose(grad_hidden, up_full))
        grad_low_two, grad_gain_two, grad_shift_two = norm_backward(
            grad_lifted, scaled_two, inverse_two, full_gains[layer_index, 1]
        )
        grad_middle = grad_stream + grad_low_two
        grad_out_shift = jnp.sum(grad_middle, axis=0)
        attn_grad = gather_grads(grad_middle.astype(jnp.bfloat16))
        grad_out = inner_rows(mixture, attn_grad)
        grad_mixture = times_transpose(attn_grad, out_full).astype(jnp.bfloat16).reshape(head_shape)
        grad_queries, grad_keys, grad_values = lax.map(
            lambda operands: attend_back(
                operands[0], operands[1], operands[2], operands[3], operands[4], block_rows
            ),
            (queries, key_rows, values, log_sum, grad_mixture),
        )
        grad_queries = grad_queries.reshape(total_rows, -1)
        grad_keys = grad_keys.reshape(total_rows, -1)
        grad_values = grad_values.reshape(total_rows, -1)
        grad_in_bias = jnp.stack(
            [
                jnp.sum(grad_queries.astype(jnp.float32), axis=0),
                jnp.sum(grad_values.astype(jnp.float32), axis=0),
            ]
        )
        grad_in = jnp.stack(
            [
                inner_rows(normed_all, grad_queries),
                inner_rows(normed_all, grad_keys),
                inner_rows(normed_all, grad_values),
            ]
        )
        grad_normed_part = (
            times_transpose(grad_queries, in_full[0])
            + times_transpose(grad_keys, in_full[1])
            + times_transpose(grad_values, in_full[2])
        )
        grad_normed = scatter_grads(grad_normed_part)
        grad_low_one, grad_gain_one, grad_shift_one = norm_backward(
            grad_normed, scaled_one, inverse_one, full_gains[layer_index, 0]
        )
        grad_stream = grad_middle + grad_low_one
        gain_grad_list[layer_index] = jnp.stack([grad_gain_one, grad_gain_two])
        shift_grad_list[layer_index] = jnp.stack(
            [grad_shift_one, grad_out_shift, grad_shift_two, grad_down_shift]
        )
        layer_grads = (
            grad_in[None],
            grad_in_bias[None],
            grad_out[None],
            grad_up[None],
            grad_up_bias[None],
            grad_down[None],
        )
        weight_grad_list[layer_index] = reduce_weights(layer_grads)
    stacked = tuple(
        (
            jnp.concatenate([weight_grad_list[index][member] for index in range(layers)], axis=0)
            for member in range(6)
        )
    )
    grad_gains, grad_shifts = (
        lax.psum_scatter(
            jnp.stack(gain_grad_list), ("dp", "tensor"), scatter_dimension=2, tiled=True
        ),
        lax.psum_scatter(
            jnp.stack(shift_grad_list), ("dp", "tensor"), scatter_dimension=2, tiled=True
        ),
    )
    return (
        stream,
        grad_stream,
        stacked[0],
        stacked[1],
        stacked[2],
        stacked[3],
        stacked[4],
        stacked[5],
        grad_gains,
        grad_shifts,
    )


def solution(mesh):
    in_specs = (
        P(("dp", "tensor"), None),
        P(("dp", "tensor"), None),
        P(None, None, "dp", "tensor"),
        P(None, None, ("tensor", "dp")),
        P(None, "tensor", "dp"),
        P(None, "dp", "tensor"),
        P(None, ("tensor", "dp")),
        P(None, "tensor", "dp"),
        P(None, None, ("dp", "tensor")),
        P(None, None, ("dp", "tensor")),
    )
    out_specs = (
        P(("dp", "tensor"), None),
        P(("dp", "tensor"), None),
        P(None, None, "dp", "tensor"),
        P(None, None, ("tensor", "dp")),
        P(None, "tensor", "dp"),
        P(None, "dp", "tensor"),
        P(None, ("tensor", "dp")),
        P(None, "tensor", "dp"),
        P(None, None, ("dp", "tensor")),
        P(None, None, ("dp", "tensor")),
    )
    return jax.shard_map(
        per_device, mesh=mesh, in_specs=in_specs, out_specs=out_specs, check_vma=False
    )
```

profile of v0, /device:TPU:22, one launch (start us, length us, event | category | flops | bytes accessed | tf_op | source)
XLA Modules:
  0.0 2408.7 jit_solution(1516330788616185812)
XLA Ops:
  12.0 36.1 %all_gather.75 = f32[2,4,768]{1,0,2:T(2,128)S(1)} all-gather(f32[2,4,6]{1,0,2:T(2,128)S(1)} %copy.40), channel_id=1, replica_groups=mesh['dp'=32,'tensor'=4] {'dp','tensor'}, dimensions={2}, use_global_device_ids=true | all-gather | bytes 24768 | tf_op jit(solution)/shard_map/all_gather | solution.py:160
  48.1 21.0 slice_reduce_fusion
  69.1 34.4 %all_gather.74 = f32[2,2,768]{1,0,2:T(2,128)S(1)} all-gather(f32[2,2,6]{1,0,2:T(2,128)S(1)} %copy.39), channel_id=1, replica_groups=mesh['dp'=32,'tensor'=4] {'dp','tensor'}, dimensions={2}, use_global_device_ids=true | all-gather | bytes 12384 | tf_op jit(solution)/shard_map/all_gather | solution.py:159
  103.4 9.7 slice_reduce_fusion.2
  114.4 82.2 %all_gather.78 = bf16[1,2,192]{1,0,2:T(2,128)(2,1)S(1)} all-gather(bf16[1,2,6]{1,0,2:T(2,128)(2,1)S(1)} %copy.67), channel_id=1, replica_groups=mesh['dp'=32,'tensor'=4] {'dp'}, dimensions={2}, use_global_device_ids=true | all-gather | bytes 792 | tf_op jit(solution)/shard_map/all_gather | solution.py:166
  199.6 93.0 %all_gather.79 = bf16[1,192,768]{1,2,0:T(8,128)(2,1)S(1)} all-gather(bf16[1,192,24]{1,2,0:T(8,128)(2,1)S(1)} %get-tuple-element.185), channel_id=1, replica_groups=mesh['dp'=32,'tensor'=4] {'dp'}, dimensions={2}, use_global_device_ids=true | all-gather | bytes 304128 | tf_op jit(solution)/shard_map/all_gather | solution.py:167
  292.6 94.1 %all_gather.77 = bf16[1,3,768,192]{3,2,1,0:T(8,128)(2,1)S(1)} all-gather(bf16[1,3,24,192]{3,2,1,0:T(8,128)(2,1)S(1)} %get-tuple-element.183), channel_id=1, replica_groups=mesh['dp'=32,'tensor'=4] {'dp'}, dimensions={2}, use_global_device_ids=true | all-gather | bytes 912384 | tf_op jit(solution)/shard_map/all_gather | solution.py:165
  403.4 42.7 %reduce-scatter.17.cloned.1.call-done = f32[256,768]{1,0:T(8,128)} async-done(((f32[1024,768]{1,0:T(8,128)}), f32[256,768]{1,0:T(8,128)}) %reduce-scatter.17.cloned.1.call-update) | async-done | bytes 786448 | tf_op jit(solution)/shard_map/reduce_scatter | solution.py:59
  451.2 86.0 %all-reduce.17 = (bf16[768]{0:T(1024)(128)(2,1)S(1)}, bf16[768]{0:T(1024)(128)(2,1)}) all-reduce(bf16[768]{0:T(1024)(128)(2,1)S(1)} %dynamic-update-slice, bf16[768]{0:T(1024)(128)(2,1)S(1)} %dynamic-update-slice.1), channel_id=1, replica_groups=mesh['dp'=32,'tensor'=4] {'dp'}, use_global_device_ids=true, to_apply=%add | all-reduce | flops 1536 | bytes 6144
  537.2 10.4 fusion.18
  547.6 32.9 %all-gather.19.cloned.1.call-done = bf16[1,768,768]{1,2,0:T(8,128)(2,1)} async-done(((bf16[1,768,24]{1,2,0:T(8,128)(2,1)}), bf16[1,768,768]{1,2,0:T(8,128)(2,1)}) %all-gather.19.cloned.1.call-update) | async-done | bytes 1179664 | tf_op jit(solution)/shard_map/all_gather | solution.py:170
  584.9 35.7 %reduce-scatter.19.cloned.1.call-done = f32[256,768]{1,0:T(8,128)} async-done(((f32[1024,768]{1,0:T(8,128)}), f32[256,768]{1,0:T(8,128)}) %reduce-scatter.19.cloned.1.call-update) | async-done | bytes 786448 | tf_op jit(solution)/shard_map/reduce_scatter | solution.py:59
  623.2 83.8 %all_gather.86 = bf16[1,2,192]{1,0,2:T(2,128)(2,1)S(1)} all-gather(bf16[1,2,6]{1,0,2:T(2,128)(2,1)S(1)} %copy.68), channel_id=1, replica_groups=mesh['dp'=32,'tensor'=4] {'dp'}, dimensions={2}, use_global_device_ids=true | all-gather | bytes 792 | tf_op jit(solution)/shard_map/all_gather | solution.py:166
  710.0 92.5 %all_gather.87 = bf16[1,192,768]{1,2,0:T(8,128)(2,1)S(1)} all-gather(bf16[1,192,24]{1,2,0:T(8,128)(2,1)S(1)} %get-tuple-element.184), channel_id=1, replica_groups=mesh['dp'=32,'tensor'=4] {'dp'}, dimensions={2}, use_global_device_ids=true | all-gather | bytes 304128 | tf_op jit(solution)/shard_map/all_gather | solution.py:167
  802.6 94.4 %all_gather.85 = bf16[1,3,768,192]{3,2,1,0:T(8,128)(2,1)S(1)} all-gather(bf16[1,3,24,192]{3,2,1,0:T(8,128)(2,1)S(1)} %get-tuple-element.182), channel_id=1, replica_groups=mesh['dp'=32,'tensor'=4] {'dp'}, dimensions={2}, use_global_device_ids=true | all-gather | bytes 912384 | tf_op jit(solution)/shard_map/all_gather | solution.py:165
  913.4 41.3 %reduce-scatter.21.cloned.1.call-done = f32[256,768]{1,0:T(8,128)} async-done(((f32[1024,768]{1,0:T(8,128)}), f32[256,768]{1,0:T(8,128)}) %reduce-scatter.21.cloned.1.call-update) | async-done | bytes 786448 | tf_op jit(solution)/shard_map/reduce_scatter | solution.py:59
  961.5 31.1 %all-gather.25.cloned.1.call-done = bf16[1,768,768]{2,1,0:T(8,128)(2,1)} async-done(((bf16[1,24,768]{2,1,0:T(8,128)(2,1)}), bf16[1,768,768]{2,1,0:T(8,128)(2,1)}) %all-gather.25.cloned.1.call-update) | async-done | bytes 1179664 | tf_op jit(solution)/shard_map/all_gather | solution.py:168
  992.6 25.8 %all-gather.23.cloned.1.call-done = bf16[1024,768]{1,0:T(8,128)(2,1)} async-done(((bf16[256,768]{1,0:T(8,128)(2,1)}), bf16[1024,768]{1,0:T(8,128)(2,1)}) %all-gather.23.cloned.1.call-update) | async-done | bytes 1572880 | tf_op jit(solution)/shard_map/all_gather | solution.py:55
  1018.4 10.6 fusion.21
  1029.0 59.4 %all-gather.27.cloned.1.call-done = bf16[1,768,768]{1,2,0:T(8,128)(2,1)} async-done(((bf16[1,768,24]{1,2,0:T(8,128)(2,1)}), bf16[1,768,768]{1,2,0:T(8,128)(2,1)}) %all-gather.27.cloned.1.call-update) | async-done | bytes 1179664 | tf_op jit(solution)/shard_map/all_gather | solution.py:170
  1088.4 25.0 %all-gather.29.cloned.1.call-done = bf16[1024,768]{1,0:T(8,128)(2,1)} async-done(((bf16[256,768]{1,0:T(8,128)(2,1)}), bf16[1024,768]{1,0:T(8,128)(2,1)}) %all-gather.29.cloned.1.call-update) | async-done | bytes 1572880 | tf_op jit(solution)/shard_map/all_gather | solution.py:63
  1128.2 33.1 %reduce-scatter.25.cloned.1.call-done = f32[256,768]{1,0:T(8,128)} async-done(((f32[1024,768]{1,0:T(8,128)}), f32[256,768]{1,0:T(8,128)}) %reduce-scatter.25.cloned.1.call-update) | async-done | bytes 786448 | tf_op jit(solution)/shard_map/reduce_scatter | solution.py:67
  1164.1 37.4 %reduce-scatter.23.cloned.1.call-done = f32[256,768]{1,0:T(8,128)} async-done(((f32[1024,768]{1,0:T(8,128)}), f32[256,768]{1,0:T(8,128)}) %reduce-scatter.23.cloned.1.call-update) | async-done | bytes 786448 | tf_op jit(solution)/shard_map/reduce_scatter | solution.py:59
  1208.2 24.0 all-gather.31.cloned.1.call-done
  1254.9 37.7 %reduce-scatter.27.cloned.1.call-done = f32[256,768]{1,0:T(8,128)} async-done(((f32[1024,768]{1,0:T(8,128)}), f32[256,768]{1,0:T(8,128)}) %reduce-scatter.27.cloned.1.call-update) | async-done | bytes 786448 | tf_op jit(solution)/shard_map/reduce_scatter | solution.py:67
  1297.9 25.7 %all-gather.33.cloned.1.call-done = bf16[1024,768]{1,0:T(8,128)(2,1)} async-done(((bf16[256,768]{1,0:T(8,128)(2,1)}), bf16[1024,768]{1,0:T(8,128)(2,1)}) %all-gather.33.cloned.1.call-update) | async-done | bytes 1572880 | tf_op jit(solution)/shard_map/all_gather | solution.py:63
  1333.3 37.7 %reduce-scatter.29.cloned.1.call-done = f32[256,768]{1,0:T(8,128)} async-done(((f32[1024,768]{1,0:T(8,128)}), f32[256,768]{1,0:T(8,128)}) %reduce-scatter.29.cloned.1.call-update) | async-done | bytes 786448 | tf_op jit(solution)/shard_map/reduce_scatter | solution.py:67
  1385.1 16.2 all-gather.35.cloned.1.call-done
  1476.3 131.9 %reduce-scatter.35.cloned.1.call-done = f32[1,24,768]{2,1,0:T(8,128)} async-done(((f32[1,768,768]{2,1,0:T(8,128)}), f32[1,24,768]{2,1,0:T(8,128)}) %reduce-scatter.35.cloned.1.call-update) | async-done | bytes 73744 | tf_op jit(solution)/shard_map/reduce_scatter | solution.py:75
  1608.2 228.5 %reduce-scatter.33.cloned.1.call-done = f32[1,24,768]{2,1,0:T(8,128)} async-done(((f32[1,768,768]{2,1,0:T(8,128)}), f32[1,24,768]{2,1,0:T(8,128)}) %reduce-scatter.33.cloned.1.call-update) | async-done | bytes 73744 | tf_op jit(solution)/shard_map/reduce_scatter | solution.py:75
  1838.6 172.9 %all-reduce.15 = (f32[1,2,192]{2,1,0:T(2,128)S(1)}, f32[1,2,192]{2,1,0:T(2,128)S(1)}, f32[1,768]{1,0:T(1,128)S(1)}, f32[1,768]{1,0:T(1,128)S(1)}) all-reduce(f32[1,2,192]{2,1,0:T(2,128)S(1)} %maximum_bitcast_fusion.7, f32[1,2,192]{2,1,0:T(2,128)S(1)} %maximum_bitcast_fusion.6, ...), channel_id=13, replica_groups=mesh['dp'=32,'tensor'=4] {'dp'}, use_global_device_ids=true, to_apply=%region_43.44.clone | all-reduce | flops 2304 | bytes 18432
  2014.6 375.5 %all-reduce.14 = (f32[2,2,768]{2,1,0:T(2,128)S(1)}, f32[2,4,768]{2,1,0:T(4,128)S(1)}) all-reduce(f32[2,2,768]{2,1,0:T(2,128)S(1)} %pad_maximum_fusion.13, f32[2,4,768]{2,1,0:T(4,128)S(1)} %pad_maximum_fusion.12), channel_id=22, replica_groups=mesh['dp'=32,'tensor'=4] {'dp','tensor'}, use_global_device_ids=true, to_apply=%region_58.59.clone | all-reduce | flops 9216 | bytes 73728
  (467 shorter events, 225.9 us)
Async XLA Ops:
  8.0 378.7 %all-gather.13.cloned.1.call-start = ((), (), s32[]{:S(2)}) async-start(), calls=%async_computation.10 | async-start | bytes 1966080 | tf_op jit(solution)/shard_map/all_gather | solution.py:55
  113.1 334.6 %copy-start.57 = (f32[768]{0:T(1024)}, f32[768]{0:T(1024)S(1)}, u32[]{:S(2)}) copy-start(f32[768]{0:T(1024)S(1)} %get-tuple-element.136) | copy-start | bytes 9220
  113.2 508.9 %copy-start.59 = (f32[768]{0:T(1024)}, f32[768]{0:T(1024)S(1)}, u32[]{:S(2)}) copy-start(f32[768]{0:T(1024)S(1)} %get-tuple-element.135) | copy-start | bytes 9220
  114.2 331.9 %reduce-scatter.17.cloned.1.call-start = ((), (), s32[]{:S(2)}) async-start(), calls=%async_computation.11 | async-start | bytes 3932160 | tf_op jit(solution)/shard_map/reduce_scatter | solution.py:59
  402.7 134.5 %all-gather.17.cloned.1.call-start = ((), (), s32[]{:S(2)}) async-start(), calls=%async_computation.13 | async-start | bytes 1216512 | tf_op jit(solution)/shard_map/all_gather | solution.py:168
  403.4 133.8 %all-gather.15.cloned.1.call-start = ((), (), s32[]{:S(2)}) async-start(), calls=%async_computation.12 | async-start | bytes 1966080 | tf_op jit(solution)/shard_map/all_gather | solution.py:55
  448.7 131.7 %all-gather.19.cloned.1.call-start = ((), (), s32[]{:S(2)}) async-start(), calls=%async_computation.14 | async-start | bytes 1216512 | tf_op jit(solution)/shard_map/all_gather | solution.py:170
  449.4 171.1 %reduce-scatter.19.cloned.1.call-start = ((), (), s32[]{:S(2)}) async-start(), calls=%async_computation.15 | async-start | bytes 3932160 | tf_op jit(solution)/shard_map/reduce_scatter | solution.py:59
  584.8 312.2 %all-gather.21.cloned.1.call-start = ((), (), s32[]{:S(2)}) async-start(), calls=%async_computation.16 | async-start | bytes 1966080 | tf_op jit(solution)/shard_map/all_gather | solution.py:55
  623.1 331.6 %reduce-scatter.21.cloned.1.call-start = ((), (), s32[]{:S(2)}) async-start(), calls=%async_computation.17 | async-start | bytes 3932160 | tf_op jit(solution)/shard_map/reduce_scatter | solution.py:59
  912.6 80.1 %all-gather.25.cloned.1.call-start = ((), (), s32[]{:S(2)}) async-start(), calls=%async_computation.19 | async-start | bytes 1216512 | tf_op jit(solution)/shard_map/all_gather | solution.py:168
  913.3 105.1 %all-gather.23.cloned.1.call-start = ((), (), s32[]{:S(2)}) async-start(), calls=%async_computation.18 | async-start | bytes 1966080 | tf_op jit(solution)/shard_map/all_gather | solution.py:55
  958.5 129.9 %all-gather.27.cloned.1.call-start = ((), (), s32[]{:S(2)}) async-start(), calls=%async_computation.20 | async-start | bytes 1216512 | tf_op jit(solution)/shard_map/all_gather | solution.py:170
  959.1 154.3 %all-gather.29.cloned.1.call-start = ((), (), s32[]{:S(2)}) async-start(), calls=%async_computation.22 | async-start | bytes 1966080 | tf_op jit(solution)/shard_map/all_gather | solution.py:63
  959.7 201.7 %reduce-scatter.25.cloned.1.call-start = ((), (), s32[]{:S(2)}) async-start(), calls=%async_computation.23 | async-start | bytes 3932160 | tf_op jit(solution)/shard_map/reduce_scatter | solution.py:67
  1123.3 78.2 %reduce-scatter.23.cloned.1.call-start = ((), (), s32[]{:S(2)}) async-start(), calls=%async_computation.21 | async-start | bytes 3932160 | tf_op jit(solution)/shard_map/reduce_scatter | solution.py:59
  1128.2 104.0 %all-gather.31.cloned.1.call-start = ((), (), s32[]{:S(2)}) async-start(), calls=%async_computation.24 | async-start | bytes 1966080 | tf_op jit(solution)/shard_map/all_gather | solution.py:63
  1206.6 86.0 %reduce-scatter.27.cloned.1.call-start = ((), (), s32[]{:S(2)}) async-start(), calls=%async_computation.25 | async-start | bytes 3932160 | tf_op jit(solution)/shard_map/reduce_scatter | solution.py:67
  1254.8 68.7 %all-gather.33.cloned.1.call-start = ((), (), s32[]{:S(2)}) async-start(), calls=%async_computation.26 | async-start | bytes 1966080 | tf_op jit(solution)/shard_map/all_gather | solution.py:63
  1297.6 73.4 %reduce-scatter.29.cloned.1.call-start = ((), (), s32[]{:S(2)}) async-start(), calls=%async_computation.27 | async-start | bytes 3932160 | tf_op jit(solution)/shard_map/reduce_scatter | solution.py:67
  1333.3 68.0 %all-gather.35.cloned.1.call-start = ((), (), s32[]{:S(2)}) async-start(), calls=%async_computation.28 | async-start | bytes 1966080 | tf_op jit(solution)/shard_map/all_gather | solution.py:63
  1374.9 233.3 %reduce-scatter.35.cloned.1.call-start = ((), (), s32[]{:S(2)}) async-start(), calls=%async_computation.31 | async-start | bytes 2433024 | tf_op jit(solution)/shard_map/reduce_scatter | solution.py:75
  1379.7 457.0 %reduce-scatter.33.cloned.1.call-start = ((), (), s32[]{:S(2)}) async-start(), calls=%async_computation.30 | async-start | bytes 2433024 | tf_op jit(solution)/shard_map/reduce_scatter | solution.py:75
  1384.6 628.3 %reduce-scatter.31.cloned.1.call-start = ((), (), s32[]{:S(2)}) async-start(), calls=%async_computation.29 | async-start | bytes 3932160 | tf_op jit(solution)/shard_map/reduce_scatter | solution.py:67
  1424.3 969.5 %all-reduce.20.cloned.1.call-start = ((), (), s32[]{:S(2)}) async-start(), calls=%async_computation.32 | async-start | bytes 22020096
  1474.2 364.1 %copy-start.89 = (f32[3,64]{1,0:T(4,128)S(1)}, f32[3,64]{1,0:T(4,128)}, u32[]{:S(2)}) copy-start(f32[3,64]{1,0:T(4,128)} %get-tuple-element.214) | copy-start | bytes 2308
  1474.2 364.2 %copy-start.37 = (bf16[3,64,512]{2,1,0:T(8,128)(2,1)S(1)}, bf16[3,64,512]{2,1,0:T(8,128)(2,1)}, u32[]{:S(2)}) copy-start(bf16[3,64,512]{2,1,0:T(8,128)(2,1)} %copy-done.36) | copy-start | bytes 589828
  1474.2 364.2 %copy-start.39 = (bf16[3,64,512]{2,1,0:T(8,128)(2,1)S(1)}, bf16[3,64,512]{2,1,0:T(8,128)(2,1)}, u32[]{:S(2)}) copy-start(bf16[3,64,512]{2,1,0:T(8,128)(2,1)} %copy-done.38) | copy-start | bytes 589828
  1474.2 538.7 %copy-start.9 = (bf16[256,768]{1,0:T(8,128)(2,1)S(1)}, bf16[256,768]{1,0:T(8,128)(2,1)}, u32[]{:S(2)}) copy-start(bf16[256,768]{1,0:T(8,128)(2,1)} %param.10) | copy-start | bytes 1179652
  1474.2 538.7 %copy-start.56 = (f32[768]{0:T(1024)S(1)}, f32[768]{0:T(1024)}, u32[]{:S(2)}) copy-start(f32[768]{0:T(1024)} %copy-done.55) | copy-start | bytes 9220
  1474.2 538.7 %copy-start.68 = (f32[256]{0:T(256)S(1)}, f32[256]{0:T(256)}, u32[]{:S(2)}) copy-start(f32[256]{0:T(256)} %copy-done.67) | copy-start | bytes 3076
  1474.3 538.7 %copy-start.76 = (f32[256]{0:T(256)S(1)}, f32[256]{0:T(256)}, u32[]{:S(2)}) copy-start(f32[256]{0:T(256)} %copy-done.75) | copy-start | bytes 3076
  (101 other events, 2572.6 us)
Sparse Core Ops, SparseCore 0:
  114.3 24.7 all-gather.12
  402.8 43.3 reduce-scatter.16
  623.2 26.0 all-gather.20
  912.7 41.9 reduce-scatter.20
  1123.4 37.8 reduce-scatter.24
  1163.6 37.8 reduce-scatter.22
  1297.7 25.7 all-gather.32
  1374.9 26.2 all-gather.34
Sparse Core Ops, SparseCore 1:
  406.7 77.5 all-gather.16
  486.4 23.8 all-gather.14
  513.6 66.7 all-gather.18
  584.9 35.6 reduce-scatter.18
  916.9 75.7 all-gather.24
  994.9 23.5 all-gather.22
  1021.8 66.6 all-gather.26
  1089.9 23.5 all-gather.28
  1206.7 25.5 all-gather.30
  1254.9 37.6 reduce-scatter.26
  1333.3 37.6 reduce-scatter.28
  1380.6 227.5 reduce-scatter.34
  1613.0 223.7 reduce-scatter.32
  1839.1 36.9 reduce-scatter.30
  1879.1 510.2 all-reduce.19
where the time goes:
time: 2420 us; the launch traced here: 2410 us
  blocking collectives  1240 us (51%)
  waiting for transfers between devices  868 us (36%)
  matrix products  138 us (6%)
  local copies, waits for them, and re-layouts  78.4 us (3%)
  other arithmetic  56.5 us (2%)
    unnamed x3, blocking collectives  634 us
    reduce_scatter x2, waiting for transfers between devices, reduce_weights(): lax.psum_scatter(grad_tuple[3], 'dp', scatter_dimension=1, tiled=True)  360 us
    all_gather x2, blocking collectives, fetch(): lax.all_gather(attention_in[layer_index:layer_index + 1], 'dp', axis=2, t...  189 us
    all_gather x2, blocking collectives, fetch(): lax.all_gather(attention_out[layer_index:layer_index + 1], 'dp', axis=2,...  186 us
    all_gather x2, blocking collectives, fetch(): lax.all_gather(attention_bias[layer_index:layer_index + 1], 'dp', axis=2,...  166 us
    reduce_scatter x4, waiting for transfers between devices, scatter_rows(): return lax.psum_scatter(values, 'tensor', scatter_dimension=0, tiled=True)  157 us
    reduce_scatter x4, waiting for transfers between devices, scatter_grads(): return lax.psum_scatter(values, 'tensor', scatter_dimension=0, tiled=True)  109 us
    all_gather x2, waiting for transfers between devices, fetch(): lax.all_gather(down_weight[layer_index:layer_index + 1], 'dp', axis=2, ti...  92.2 us
  transfers between devices with their start and end apart: 23, of which 17 were waited for; matrix products, arithmetic and copies ran while one was open for 6% of the time, Pallas kernels for 0%

commit v1 on v0

v1 whole, which is shorter than its diff:
```python
import jax
import jax.numpy as jnp
from jax import lax
from jax.sharding import Mesh, PartitionSpec as P

HEAD_DIM = 64
D = 768
bf16 = jnp.bfloat16
f32 = jnp.float32

norm_eps = 1e-05
score_scale = 0.125
root_half = 0.7071067811865476
inv_root_two_pi = 0.3989422804014327

CHIPS = ("x", "y", "zh", "zl")
ALL = CHIPS + ("core",)
RING = {"x": "x", "y": "y", "z": ("zh", "zl")}


def norm_forward(stream, gain_row, shift_row):
    row_mean = jnp.mean(stream, axis=-1, keepdims=True)
    centred = stream - row_mean
    variance = jnp.mean(centred * centred, axis=-1, keepdims=True)
    inverse = lax.rsqrt(variance + norm_eps)
    scaled = centred * inverse
    return (scaled * gain_row + shift_row, scaled, inverse)


def norm_backward(grad_output, scaled, inverse, gain_row):
    grad_scaled = grad_output * gain_row
    mean_grad = jnp.mean(grad_scaled, axis=-1, keepdims=True)
    mean_cross = jnp.mean(grad_scaled * scaled, axis=-1, keepdims=True)
    grad_input = inverse * (grad_scaled - mean_grad - scaled * mean_cross)
    return (grad_input, jnp.sum(grad_output * scaled, axis=0), jnp.sum(grad_output, axis=0))


def gelu_slope(hidden):
    normal_cdf = 0.5 * (1.0 + lax.erf(hidden * root_half))
    return normal_cdf + hidden * jnp.exp(-0.5 * hidden * hidden) * inv_root_two_pi


def dot(left, right, left_dim, right_dim):
    return lax.dot_general(
        left, right, (((left_dim,), (right_dim,)), ((), ())), preferred_element_type=f32
    )


def split_low(value):
    high = lax.reduce_precision(value, 8, 7)
    return high.astype(bf16), (value - high).astype(bf16)


def core_gather(value):
    return lax.all_gather(value, "core", axis=0, tiled=True)


def core_scatter(partial):
    rows = partial.shape[0] // 2
    core = lax.axis_index("core")
    away = lax.dynamic_slice_in_dim(partial, (1 - core) * rows, rows, 0).astype(bf16)
    kept = lax.dynamic_slice_in_dim(partial, core * rows, rows, 0)
    return kept + lax.ppermute(away, "core", [(0, 1), (1, 0)]).astype(f32)


def swap_zl(value):
    return lax.ppermute(value, "zl", [(0, 1), (1, 0)])


def halve(value, axis):
    me = lax.axis_index(RING[axis])
    pick = lambda index: lax.dynamic_index_in_dim(value, index, 0, False)
    near = [(i, i ^ 1) for i in range(4)]
    far = [(i, i ^ 3) for i in range(4)]
    if axis == "z":
        near, far, one, three = far, near, 3, 1
    else:
        one, three = 1, 3
    sent = jnp.stack([pick(me ^ one), pick(me ^ 2)])
    came = lax.ppermute(sent, RING[axis], near)
    onward = (pick(me ^ three).astype(f32) + came[1].astype(f32)).astype(bf16)
    last = lax.ppermute(onward, RING[axis], far)
    return pick(me).astype(f32) + came[0].astype(f32) + last.astype(f32)


def reduce_stream(value, order):
    dims = ["x", "y", "z"]
    for step, axis in enumerate(order):
        value = halve(jnp.moveaxis(value, dims.index(axis), 0), axis)
        dims.remove(axis)
        if step < 2:
            value = value.astype(bf16)
    return value


def place_stream(halves):
    rows = D // 32
    parts = [half.reshape(4, 4, 2, 1, rows, half.shape[1]) for half in halves]
    return jnp.concatenate(parts, axis=3).reshape(4, 4, 4, rows, halves[0].shape[1])


def attend(queries, key_rows, values):
    scores = jnp.einsum("qhd,khd->hqk", queries, key_rows, preferred_element_type=f32)
    scores = scores * score_scale
    row_max = jnp.max(scores, axis=-1, keepdims=True)
    shifted = jnp.exp(scores - row_max)
    total = jnp.sum(shifted, axis=-1, keepdims=True)
    attention = (shifted / total).astype(bf16)
    mixture = jnp.einsum("hqk,khd->qhd", attention, values, preferred_element_type=f32)
    return mixture.astype(bf16), row_max + jnp.log(total)


def attend_back(queries, key_rows, values, log_sum, grad_mixture):
    scores = jnp.einsum("qhd,khd->hqk", queries, key_rows, preferred_element_type=f32)
    attention = jnp.exp(scores * score_scale - log_sum)
    grad_attention = jnp.einsum("qhd,khd->hqk", grad_mixture, values, preferred_element_type=f32)
    row_delta = jnp.sum(attention * grad_attention, axis=-1, keepdims=True)
    grad_scores = (attention * (grad_attention - row_delta)).astype(bf16)
    grad_queries = jnp.einsum("hqk,khd->qhd", grad_scores, key_rows, preferred_element_type=f32)
    grad_keys = jnp.einsum("hqk,qhd->khd", grad_scores, queries, preferred_element_type=f32)
    grad_values = jnp.einsum(
        "hqk,qhd->khd", attention.astype(bf16), grad_mixture, preferred_element_type=f32
    )
    return grad_queries * score_scale, grad_keys * score_scale, grad_values


def per_device(
    input_frames,
    cotangent,
    attention_in,
    attention_bias,
    attention_out,
    up_weight,
    up_bias,
    down_weight,
    norm_gains,
    row_shifts,
):
    layers = attention_in.shape[0]
    core = lax.axis_index("core")
    rows = D // 32

    gains_shifts = jnp.concatenate([norm_gains.reshape(4, 6), row_shifts.reshape(8, 6)], axis=0)
    both_cores = lax.all_gather(gains_shifts, "core", axis=0)
    high, low = split_low(both_cores)
    small = jnp.concatenate([high[0], low[0], high[1], low[1]], axis=1)
    biases = jnp.concatenate([attention_bias.reshape(4, 6), up_bias.reshape(8, 6)], axis=0)
    small = jnp.concatenate([small, jnp.pad(biases, ((0, 0), (0, 18)))], axis=0)
    small = jnp.pad(small, ((0, 0), (0, 104)))

    def packed(layer):
        return jnp.concatenate(
            [
                down_weight[layer].T,
                up_weight[layer],
                attention_in[layer, 0],
                attention_in[layer, 1],
                attention_in[layer, 2],
                attention_out[layer].T,
            ],
            axis=1,
        )

    gathered = []
    for layer in range(layers):
        block = packed(layer)
        if layer == 0:
            block = jnp.concatenate([block, small], axis=1)
        whole = lax.all_gather(block, CHIPS, axis=0, tiled=True)
        gathered.append(whole.reshape(32, 2, rows, block.shape[1]))

    def columns(layer, first, last):
        halves = [gathered[layer][:, z, :, first:last].reshape(D, last - first) for z in range(2)]
        return jnp.concatenate(halves, axis=1)

    tiny = gathered[0][:, :, :, 2304:2328].astype(f32)
    by_core = tiny[:, :, :12].reshape(32, 2, 12, 2, 2, 6)
    full = (by_core[:, :, :, :, 0] + by_core[:, :, :, :, 1]).transpose(2, 0, 1, 3, 4).reshape(12, D)
    full_gains = full[:4].reshape(2, 2, D)
    full_shifts = full[4:].reshape(2, 4, D)
    in_bias = tiny[:, :, 12:16, :6].transpose(2, 1, 0, 3).reshape(2, 2, 2, 192)
    hidden_bias = tiny[:, :, 16:24, :6].reshape(32, 2, 2, 24).transpose(2, 1, 0, 3).reshape(2, 1536)

    def heads(qkv_part):
        return qkv_part.reshape(qkv_part.shape[0], 6, HEAD_DIM)

    stream = input_frames.astype(f32)
    stored = []
    for layer in range(layers):
        w_down = columns(layer, 0, 768)
        w_up = columns(layer, 768, 1536)
        w_qkv = columns(layer, 1536, 2112)
        w_out = columns(layer, 2112, 2304)
        zeros = jnp.zeros((192,), f32)
        qkv_bias = jnp.concatenate(
            [
                in_bias[layer, 0, 0],
                zeros,
                in_bias[layer, 1, 0],
                in_bias[layer, 0, 1],
                zeros,
                in_bias[layer, 1, 1],
            ]
        )
        normed, scaled_one, inverse_one = norm_forward(
            stream, full_gains[layer, 0], full_shifts[layer, 0]
        )
        normed_all = core_gather(normed.astype(bf16))
        qkv = (dot(normed_all, w_qkv, 1, 0) + qkv_bias).astype(bf16)
        queries = jnp.concatenate([qkv[:, 0:192], qkv[:, 576:768]], axis=1)
        pair = jnp.concatenate(
            [qkv[:, 192:384], qkv[:, 768:960], qkv[:, 384:576], qkv[:, 960:1152]], axis=1
        )
        pair_all = jnp.concatenate([pair, swap_zl(pair)], axis=0)
        key_rows, values = pair_all[:, :384], pair_all[:, 384:]
        mixture, log_sum = attend(heads(queries), heads(key_rows), heads(values))
        mixture = mixture.reshape(-1, 384)
        middle = stream + core_scatter(dot(mixture, w_out, 1, 1)) + full_shifts[layer, 1]
        lifted, scaled_two, inverse_two = norm_forward(
            middle, full_gains[layer, 1], full_shifts[layer, 2]
        )
        lifted_all = core_gather(lifted.astype(bf16))
        hidden = dot(lifted_all, w_up, 1, 0) + hidden_bias[layer]
        active = jax.nn.gelu(hidden, approximate=False).astype(bf16)
        stream = middle + core_scatter(dot(active, w_down, 1, 1)) + full_shifts[layer, 3]
        stored.append(
            (
                (w_down, w_up, w_qkv, w_out),
                normed_all,
                scaled_one,
                inverse_one,
                queries,
                key_rows,
                values,
                log_sum,
                mixture,
                scaled_two,
                inverse_two,
                lifted_all,
                hidden,
                active,
            )
        )

    grad_stream = cotangent.astype(f32)
    reduced = [None] * layers
    for layer in reversed(range(layers)):
        (
            (w_down, w_up, w_qkv, w_out),
            normed_all,
            scaled_one,
            inverse_one,
            queries,
            key_rows,
            values,
            log_sum,
            mixture,
            scaled_two,
            inverse_two,
            lifted_all,
            hidden,
            active,
        ) = stored[layer]
        grad_down_shift = jnp.sum(grad_stream, axis=0)
        branch_grad = core_gather(grad_stream.astype(bf16))
        grad_down = [dot(branch_grad, active[:, z * 768 : z * 768 + 768], 0, 0).astype(bf16) for z in range(2)]
        grad_active = dot(branch_grad, w_down, 1, 0)
        grad_hidden = (grad_active * gelu_slope(hidden)).astype(bf16)
        grad_up_bias = jnp.sum(grad_hidden.astype(f32), axis=0)
        grad_up = [dot(lifted_all, grad_hidden[:, z * 768 : z * 768 + 768], 0, 0).astype(bf16) for z in range(2)]
        down_sum = reduce_stream(place_stream(grad_down), "xyz")
        up_sum = reduce_stream(place_stream(grad_up), "yzx")
        grad_lifted = core_scatter(dot(grad_hidden, w_up, 1, 1))
        grad_low_two, grad_gain_two, grad_shift_two = norm_backward(
            grad_lifted, scaled_two, inverse_two, full_gains[layer, 1]
        )
        grad_middle = grad_stream + grad_low_two
        grad_out_shift = jnp.sum(grad_middle, axis=0)
        attn_grad = core_gather(grad_middle.astype(bf16))
        grad_out = [dot(attn_grad, mixture[:, z * 192 : z * 192 + 192], 0, 0) for z in range(2)]
        grad_mixture = dot(attn_grad, w_out, 1, 0).astype(bf16)
        grad_queries, grad_keys, grad_values = attend_back(
            heads(queries), heads(key_rows), heads(values), log_sum, heads(grad_mixture)
        )
        grad_queries = grad_queries.astype(bf16).reshape(-1, 384)
        grad_pair = jnp.concatenate([grad_keys.reshape(-1, 384), grad_values.reshape(-1, 384)], axis=1)
        own = grad_pair.shape[0] // 2
        grad_pair = (grad_pair[:own] + swap_zl(grad_pair[own:].astype(bf16)).astype(f32)).astype(bf16)
        grad_keys, grad_values = grad_pair[:, :384], grad_pair[:, 384:]
        grad_qkv = [
            jnp.concatenate(
                [part[:, z * 192 : z * 192 + 192] for part in (grad_queries, grad_keys, grad_values)],
                axis=1,
            )
            for z in range(2)
        ]
        grad_in = [dot(normed_all, part, 0, 0) for part in grad_qkv]
        grad_normed = core_scatter(dot(jnp.concatenate(grad_qkv, axis=1), w_qkv, 1, 1))
        grad_low_one, grad_gain_one, grad_shift_one = norm_backward(
            grad_normed, scaled_one, inverse_one, full_gains[layer, 0]
        )
        grad_stream = grad_middle + grad_low_one

        vectors = jnp.stack(
            [
                grad_gain_one,
                grad_gain_two,
                grad_shift_one,
                grad_out_shift,
                grad_shift_two,
                grad_down_shift,
            ]
        )
        vectors = lax.psum(vectors, "core").reshape(6, 32, 2, 2, 6)
        vectors = lax.dynamic_index_in_dim(vectors, core, 3, False).transpose(1, 2, 0, 3)
        bias_sums = jnp.stack(
            [
                jnp.sum(grad_queries.astype(f32), axis=0),
                jnp.sum(grad_values.astype(f32), axis=0),
            ]
        )
        bias_sums = bias_sums.reshape(2, 2, 32, 6).transpose(2, 1, 0, 3)
        up_sums = grad_up_bias.reshape(2, 32, 24).transpose(1, 0, 2)
        vectors = jnp.concatenate(
            [vectors.reshape(32, 2, 36), bias_sums.reshape(32, 2, 12), up_sums], axis=2
        ).reshape(32, 2, 24, 3)
        high, low = split_low(vectors)
        vectors = jnp.pad(jnp.concatenate([high, low], axis=3), ((0, 0), (0, 0), (0, 0), (0, 122)))
        attn_parts = [
            jnp.concatenate(
                [grad_in[z].astype(bf16), grad_out[z].astype(bf16), vectors[:, z].reshape(D, 128)],
                axis=1,
            )
            for z in range(2)
        ]
        attn_sum = reduce_stream(place_stream(attn_parts), "zxy")
        reduced[layer] = (down_sum, up_sum, attn_sum)

    grad_down = jnp.stack([part[0].T for part in reduced])
    grad_up = jnp.stack([part[1] for part in reduced])
    attn = jnp.stack([part[2] for part in reduced])
    grad_in = attn[:, :, :576].reshape(layers, rows, 3, 192).transpose(0, 2, 1, 3)
    grad_out = attn[:, :, 576:768].transpose(0, 2, 1)
    vectors = (attn[:, :, 768:771] + attn[:, :, 771:774]).reshape(layers, 72)
    grad_gains = vectors[:, :12].reshape(layers, 2, 6)
    grad_shifts = vectors[:, 12:36].reshape(layers, 4, 6)
    grad_in_bias = vectors[:, 36:48].reshape(layers, 2, 6)
    grad_up_bias = vectors[:, 48:72]
    return (
        stream,
        grad_stream,
        grad_in,
        grad_in_bias,
        grad_out,
        grad_up,
        grad_up_bias,
        grad_down,
        grad_gains,
        grad_shifts,
    )


def solution(mesh):
    chips = Mesh(mesh.devices.reshape(4, 4, 2, 2, 2), ALL)
    dp, tensor = ("x", "y", "zh"), ("zl", "core")
    both = dp + tensor
    in_specs = (
        P(both, None),
        P(both, None),
        P(None, None, dp, tensor),
        P(None, None, tensor + dp),
        P(None, tensor, dp),
        P(None, dp, tensor),
        P(None, tensor + dp),
        P(None, tensor, dp),
        P(None, None, both),
        P(None, None, both),
    )
    out_specs = (P(both, None), P(both, None)) + in_specs[2:]
    return jax.shard_map(
        per_device, mesh=chips, in_specs=in_specs, out_specs=out_specs, check_vma=False
    )
```

time: 2420 us -> 634 us (0.26)
  blocking collectives: 1240 us -> 27.7 us
  waiting for transfers between devices: 868 us -> 216 us
  starting transfers between devices: 2.41 us -> 51.1 us
  other arithmetic: 56.5 us -> 93.8 us
  matrix products: 138 us -> 101 us
  local copies, waits for them, and re-layouts: 78.4 us -> 115 us
    unnamed x3 -> x0, blocking collectives: 634 us -> none
    reduce_scatter x10 -> x0, waiting for transfers between devices: 626 us -> none  [the longest x2 360 us: reduce_weights(): lax.psum_scatter(grad_tuple[3], 'dp', scatter_dimension=1, tiled=True)]
    all_gather x8 -> x9, blocking collectives: 611 us -> 22.3 us  [the longest x8 20.5 us: core_gather(): return lax.all_gather(value, 'core', axis=0, tiled=True)]
    all_gather x12 -> x2, waiting for transfers between devices: 240 us -> 82.8 us  [per_device(): whole = lax.all_gather(block, CHIPS, axis=0, tiled=True)]
    ppermute x0 -> x48, waiting for transfers between devices: none -> 133 us  [the longest x18 52.9 us: halve(): last = lax.ppermute(onward, RING[axis], far)]
    ppermute x0 -> x48, starting transfers between devices: none -> 51 us  [the longest x18 25.7 us: halve(): came = lax.ppermute(sent, RING[axis], near)]
    dot_general x56 -> x42, matrix products: 134 us -> 96.6 us  [the longest x32 64.4 us: dot(): lax.dot_general(left, right, (((left_dim,), (right_dim,)), ((), ())), pre...]
    broadcast_in_dim x8 -> x0, local copies, waits for them, and re-layouts: 28.4 us -> none  [the longest x2 13.5 us: per_device(): grad_down[None]]
  transfers between devices with their start and end apart: 23 -> 50, of which waited for: 17 -> 22; matrix products, arithmetic and copies ran while one was open for 6% -> 38% of each run, Pallas kernels for 0% -> 0%
where the time goes in v1:
time: 634 us; the launch traced here: 622 us
  waiting for transfers between devices  216 us (34%)
  local copies, waits for them, and re-layouts  115 us (18%)
  matrix products  101 us (16%)
  other arithmetic  93.8 us (15%)
  starting transfers between devices  51.1 us (8%)
  blocking collectives  27.7 us (4%)
  between operations  17.1 us (3%)
    all_gather x2, waiting for transfers between devices, per_device(): whole = lax.all_gather(block, CHIPS, axis=0, tiled=True)  82.8 us
    dot_general x32, matrix products, dot(): lax.dot_general(left, right, (((left_dim,), (right_dim,)), ((), ())), pre...  64.4 us
    ppermute x18, waiting for transfers between devices, halve(): last = lax.ppermute(onward, RING[axis], far)  52.9 us
    ppermute x18, waiting for transfers between devices, halve(): came = lax.ppermute(sent, RING[axis], near)  52.5 us
    ppermute x4, waiting for transfers between devices, swap_zl(): return lax.ppermute(value, 'zl', [(0, 1), (1, 0)])  26.6 us
    ppermute x18, starting transfers between devices, halve(): came = lax.ppermute(sent, RING[axis], near)  25.7 us
    ppermute x18, starting transfers between devices, halve(): last = lax.ppermute(onward, RING[axis], far)  22.5 us
    all_gather x8, blocking collectives, core_gather(): return lax.all_gather(value, 'core', axis=0, tiled=True)  20.5 us
  transfers between devices with their start and end apart: 50, of which 22 were waited for; matrix products, arithmetic and copies ran while one was open for 38% of the time, Pallas kernels for 0%

profile of v1, /device:TPU:22, one launch (start us, length us, event | category | flops | bytes accessed | tf_op | source)
XLA Modules:
  0.0 622.4 jit_solution(16341565932928638609)
XLA Ops:
  18.8 74.7 %all-gather.5.cloned.1.call-done = bf16[1536,2432]{1,0:T(8,128)(2,1)} async-done(((bf16[24,2432]{1,0:T(8,128)(2,1)}), bf16[1536,2432]{1,0:T(8,128)(2,1)}) %all-gather.5.cloned.1.call-update) | async-done | bytes 7471120 | tf_op jit(solution)/shard_map/all_gather | solution.py:169
  110.5 17.4 %collective-permute-done = bf16[512,768]{1,0:T(8,128)(2,1)} collective-permute-done((bf16[512,768]{1,0:T(8,128)(2,1)}, bf16[512,768]{1,0:T(8,128)(2,1)}, u32[]{:S(2)}, u32[]{:S(2)}) %collective-permute-start) | collective-permute-done | bytes 786464 | tf_op jit(solution)/shard_map/ppermute | solution.py:67
  132.1 2.8 fusion
  136.8 3.6 fusion.74
  149.0 9.7 %fusion.17 = (bf16[512,1536]{1,0:T(8,128)(2,1)S(1)}, f32[512,1536]{1,0:T(8,128)}) fusion(f32[1536]{0:T(1024)S(1)} %add.615, bf16[512,768]{1,0:T(8,128)(2,1)S(1)} %all_gather.40, bf16[768,768]{1,0:T(8,128)(2,1)S(1)} %bitcast.524, bf16[768,768]{1,0:T(8,128)(2,1)S(1)} %bitcast.526), kind=kOutput, calls=%fused_computation.37 | convolution fusion | flops 1264582656 | bytes 7870464 | tf_op jit(solution)/shard_map/dot_general | solution.py:44
  162.9 8.1 %all-gather.7.cloned.1.call-done = bf16[1536,2304]{1,0:T(8,128)(2,1)} async-done(((bf16[24,2304]{1,0:T(8,128)(2,1)}), bf16[1536,2304]{1,0:T(8,128)(2,1)}) %all-gather.7.cloned.1.call-update) | async-done | bytes 7077904 | tf_op jit(solution)/shard_map/all_gather | solution.py:169
  187.5 4.6 fusion.208
  193.2 9.2 %collective-permute-done.3 = bf16[512,768]{1,0:T(8,128)(2,1)} collective-permute-done((bf16[512,768]{1,0:T(8,128)(2,1)}, bf16[512,768]{1,0:T(8,128)(2,1)}, u32[]{:S(2)}, u32[]{:S(2)}) %collective-permute-start.3) | collective-permute-done | bytes 786464 | tf_op jit(solution)/shard_map/ppermute | solution.py:67
  213.4 3.6 fusion.73
  220.4 2.8 all_gather.43
  223.3 7.7 %fusion.20 = (bf16[512,1536]{1,0:T(8,128)(2,1)S(1)}, f32[512,1536]{1,0:T(8,128)S(1)}) fusion(f32[1536]{0:T(1024)S(1)} %copy-done.140, bf16[512,768]{1,0:T(8,128)(2,1)S(1)} %all_gather.43, bf16[768,768]{1,0:T(8,128)(2,1)S(1)} %bitcast.536, bf16[768,768]{1,0:T(8,128)(2,1)S(1)} %bitcast.538), kind=kOutput, calls=%fused_computation.40 | convolution fusion | flops 1264582656 | bytes 7870464 | tf_op jit(solution)/shard_map/dot_general | solution.py:44
  231.0 3.5 convert_reduce_fusion
  267.9 3.0 fusion.6
  270.9 6.4 %multiply_reduce_fusion.1 = (f32[6,512]{1,0:T(8,128)S(1)}, f32[6,512,1024]{2,1,0:T(8,128)}) fusion(f32[6,512,1024]{2,1,0:T(8,128)S(1)} %bitcast.448, f32[6,512]{1,0:T(8,128)S(1)} %copy-done.86, bf16[512,6,64]{0,2,1:T(8,128)(2,1)S(1)} %bitcast.523, bf16[1024,6,64]{0,2,1:T(8,128)(2,1)S(1)} %bitcast.497), kind=kOutput, calls=%fused_computation.4 | convolution fusion | flops 415233024 | bytes 26370048 | tf_op jit(solution)/shard_map/qhd,khd->hqk/dot_general | solution.py:116
  277.4 6.5 %multiply_convert_fusion.1 = bf16[6,512,1024]{2,1,0:T(8,128)(2,1)S(1)} fusion(f32[6,512,1024]{2,1,0:T(8,128)} %get-tuple-element.231, f32[6,512,1024]{2,1,0:T(8,128)S(1)} %bitcast.448, f32[6,512]{1,0:T(8,128)S(1)} %get-tuple-element.230, f32[6,512]{1,0:T(8,128)S(1)} %copy-done.86), kind=kLoop, calls=%fused_computation.3 | loop fusion | flops 15728640 | bytes 31481856 | tf_op jit(solution)/shard_map/convert_element_type | solution.py:118
  326.3 2.8 convert_reduce_fusion.1
  373.3 6.5 %multiply_reduce_fusion = (f32[6,512]{1,0:T(8,128)S(1)}, f32[6,512,1024]{2,1,0:T(8,128)}) fusion(f32[6,512,1024]{2,1,0:T(8,128)S(1)} %bitcast.446, f32[6,512]{1,0:T(8,128)S(1)} %log_add_fusion, bf16[512,6,64]{0,2,1:T(8,128)(2,1)S(1)} %bitcast.521, bf16[1024,6,64]{0,2,1:T(8,128)(2,1)S(1)} %bitcast.495), kind=kOutput, calls=%fused_computation.1 | convolution fusion | flops 415233024 | bytes 26370048 | tf_op jit(solution)/shard_map/qhd,khd->hqk/dot_general | solution.py:116
  379.8 6.5 %multiply_convert_fusion = bf16[6,512,1024]{2,1,0:T(8,128)(2,1)S(1)} fusion(f32[6,512,1024]{2,1,0:T(8,128)} %get-tuple-element.235, f32[6,512,1024]{2,1,0:T(8,128)S(1)} %bitcast.446, f32[6,512]{1,0:T(8,128)S(1)} %get-tuple-element.234, f32[6,512]{1,0:T(8,128)S(1)} %log_add_fusion), kind=kLoop, calls=%fused_computation | loop fusion | flops 15728640 | bytes 31481856 | tf_op jit(solution)/shard_map/convert_element_type | solution.py:118
  404.4 16.4 %collective-permute-done.33 = bf16[4,24,768]{2,1,0:T(8,128)(2,1)S(1)} collective-permute-done((bf16[4,24,768]{2,1,0:T(8,128)(2,1)S(1)}, bf16[4,24,768]{2,1,0:T(8,128)(2,1)S(1)}, u32[]{:S(2)}, u32[]{:S(2)}) %collective-permute-start.33) | collective-permute-done | bytes 147488 | tf_op jit(solution)/shard_map/ppermute | solution.py:82
  456.0 5.4 all-reduce.4
  463.8 2.9 fusion.211
  469.6 2.8 maximum_maximum_fusion.1
  476.5 3.9 fusion.212
  480.4 3.2 copy.196
  483.6 3.1 copy.199
  486.7 2.8 maximum_maximum_fusion
  500.6 43.0 %collective-permute-done.26 = bf16[2,4,24,768]{3,2,1,0:T(8,128)(2,1)S(1)} collective-permute-done((bf16[2,4,24,768]{3,2,1,0:T(8,128)(2,1)S(1)}, bf16[2,4,24,768]{3,2,1,0:T(8,128)(2,1)S(1)}, u32[]{:S(2)}, u32[]{:S(2)}) %collective-permute-start.26) | collective-permute-done | bytes 294944 | tf_op jit(solution)/shard_map/ppermute | solution.py:80
  544.8 4.0 collective-permute-done.27
  560.6 14.8 %collective-permute-done.19 = bf16[4,4,24,896]{3,2,1,0:T(8,128)(2,1)S(1)} collective-permute-done((bf16[4,4,24,896]{3,2,1,0:T(8,128)(2,1)S(1)}, bf16[4,4,24,896]{3,2,1,0:T(8,128)(2,1)S(1)}, u32[]{:S(2)}, u32[]{:S(2)}) %collective-permute-start.19) | collective-permute-done | bytes 688160 | tf_op jit(solution)/shard_map/ppermute | solution.py:82
  578.2 8.3 %collective-permute-done.13 = bf16[4,4,24,896]{3,2,1,0:T(8,128)(2,1)S(1)} collective-permute-done((bf16[4,4,24,896]{3,2,1,0:T(8,128)(2,1)S(1)}, bf16[4,4,24,896]{3,2,1,0:T(8,128)(2,1)S(1)}, u32[]{:S(2)}, u32[]{:S(2)}) %collective-permute-start.13) | collective-permute-done | bytes 688160 | tf_op jit(solution)/shard_map/ppermute | solution.py:82
  590.7 3.5 collective-permute-done.14
  601.1 2.9 collective-permute-start.16
  (715 shorter events, 308.7 us)
Async XLA Ops:
  7.2 86.3 %all-gather.5.cloned.1.call-start = ((), (), s32[]{:S(2)}) async-start(), calls=%async_computation | async-start | bytes 7587840 | tf_op jit(solution)/shard_map/all_gather | solution.py:169
  15.6 155.5 %all-gather.7.cloned.1.call-start = ((), (), s32[]{:S(2)}) async-start(), calls=%async_computation.1 | async-start | bytes 7188480 | tf_op jit(solution)/shard_map/all_gather | solution.py:169
  106.6 21.3 %collective-permute-start = (bf16[512,768]{1,0:T(8,128)(2,1)}, bf16[512,768]{1,0:T(8,128)(2,1)}, u32[]{:S(2)}, u32[]{:S(2)}) collective-permute-start(bf16[512,768]{1,0:T(8,128)(2,1)} %pad_maximum_fusion.32), channel_id=1, source_target_pairs={{0,2},{2,0},{1,3},{3,1},{4,6},{6,4},{5,7},{7,5},{8,10},{10,8},{9,1... | collective-permute-start | bytes 2359304 | tf_op jit(solution)/shard_map/ppermute | solution.py:67
  162.5 11.8 %collective-permute-start.2 = (bf16[256,768]{1,0:T(8,128)(2,1)S(1)}, bf16[256,768]{1,0:T(8,128)(2,1)S(1)}, u32[]{:S(2)}, u32[]{:S(2)}) collective-permute-start(bf16[256,768]{1,0:T(8,128)(2,1)S(1)} %dynamic-slice_convert_fusion.6), channel_id=1, source_target_pairs={{0,1},{1,0},{2,3},{3,2},{4,5},{5,4},{6,7},{7,6},{8,9},{9,8},{10,11... | collective-permute-start | bytes 1179656 | tf_op jit(solution)/shard_map/ppermute | solution.py:63
  182.5 19.9 %collective-permute-start.3 = (bf16[512,768]{1,0:T(8,128)(2,1)}, bf16[512,768]{1,0:T(8,128)(2,1)}, u32[]{:S(2)}, u32[]{:S(2)}) collective-permute-start(bf16[512,768]{1,0:T(8,128)(2,1)} %pad_maximum_fusion.33), channel_id=1, source_target_pairs={{0,2},{2,0},{1,3},{3,1},{4,6},{6,4},{5,7},{7,5},{8,10},{10,8},{9,1... | collective-permute-start | bytes 2359304 | tf_op jit(solution)/shard_map/ppermute | solution.py:67
  252.4 10.6 %collective-permute-start.5 = (bf16[256,768]{1,0:T(8,128)(2,1)S(1)}, bf16[256,768]{1,0:T(8,128)(2,1)S(1)}, u32[]{:S(2)}, u32[]{:S(2)}) collective-permute-start(bf16[256,768]{1,0:T(8,128)(2,1)S(1)} %dynamic-slice_convert_fusion.4), channel_id=1, source_target_pairs={{0,1},{1,0},{2,3},{3,2},{4,5},{5,4},{6,7},{7,6},{8,9},{9,8},{10,11... | collective-permute-start | bytes 1179656 | tf_op jit(solution)/shard_map/ppermute | solution.py:63
  252.6 9.4 %collective-permute-start.6 = (bf16[256,768]{1,0:T(8,128)(2,1)S(1)}, bf16[256,768]{1,0:T(8,128)(2,1)S(1)}, u32[]{:S(2)}, u32[]{:S(2)}) collective-permute-start(bf16[256,768]{1,0:T(8,128)(2,1)S(1)} %dynamic-slice_convert_fusion.3), channel_id=1, source_target_pairs={{0,1},{1,0},{2,3},{3,2},{4,5},{5,4},{6,7},{7,6},{8,9},{9,8},{10,11... | collective-permute-start | bytes 1179656 | tf_op jit(solution)/shard_map/ppermute | solution.py:63
  258.7 42.2 %collective-permute-start.30 = (bf16[2,4,4,24,768]{4,3,1,2,0:T(8,128)(2,1)}, bf16[2,4,4,24,768]{4,3,1,2,0:T(8,128)(2,1)}, u32[]{:S(2)}, u32[]{:S(2)}) collective-permute-start(bf16[2,4,4,24,768]{4,3,1,2,0:T(8,128)(2,1)} %pad_maximum_fusion.25), channel_id=1, source_target_pairs={{0,8},{8,0},{16,24},{24,16},{1,9},{9,1},{17,25},{25,17},{2,10},{10... | collective-permute-start | bytes 3538952 | tf_op jit(solution)/shard_map/ppermute | solution.py:80
  261.2 42.7 %collective-permute-start.42 = (bf16[2,4,4,24,768]{4,3,2,1,0:T(8,128)(2,1)}, bf16[2,4,4,24,768]{4,3,2,1,0:T(8,128)(2,1)}, u32[]{:S(2)}, u32[]{:S(2)}) collective-permute-start(bf16[2,4,4,24,768]{4,3,2,1,0:T(8,128)(2,1)} %pad_maximum_fusion.27), channel_id=1, source_target_pairs={{0,32},{32,0},{64,96},{96,64},{1,33},{33,1},{65,97},{97,65},{2,34}... | collective-permute-start | bytes 3538952 | tf_op jit(solution)/shard_map/ppermute | solution.py:80
  286.1 20.8 %collective-permute-start.7 = (bf16[512,768]{0,1:T(8,128)(2,1)}, bf16[512,768]{0,1:T(8,128)(2,1)}, u32[]{:S(2)}, u32[]{:S(2)}) collective-permute-start(bf16[512,768]{0,1:T(8,128)(2,1)} %fusion.60), channel_id=1, source_target_pairs={{0,2},{2,0},{1,3},{3,1},{4,6},{6,4},{5,7},{7,5},{8,10},{10,8},{9,1... | collective-permute-start | bytes 2359304 | tf_op jit(solution)/shard_map/ppermute | solution.py:67
  303.1 53.2 %collective-permute-start.31 = (bf16[4,4,24,768]{3,2,0,1:T(8,128)(2,1)}, bf16[4,4,24,768]{3,2,0,1:T(8,128)(2,1)}, u32[]{:S(2)}, u32[]{:S(2)}) collective-permute-start(bf16[4,4,24,768]{3,2,0,1:T(8,128)(2,1)} %fusion.75), channel_id=1, source_target_pairs={{0,24},{8,16},{16,8},{24,0},{1,25},{9,17},{17,9},{25,1},{2,26},{10... | collective-permute-start | bytes 1769480 | tf_op jit(solution)/shard_map/ppermute | solution.py:82
  306.1 55.0 %collective-permute-start.43 = (bf16[4,4,24,768]{3,2,1,0:T(8,128)(2,1)}, bf16[4,4,24,768]{3,2,1,0:T(8,128)(2,1)}, u32[]{:S(2)}, u32[]{:S(2)}) collective-permute-start(bf16[4,4,24,768]{3,2,1,0:T(8,128)(2,1)} %fusion.109), channel_id=1, source_target_pairs={{0,96},{32,64},{64,32},{96,0},{1,97},{33,65},{65,33},{97,1},{2,98}... | collective-permute-start | bytes 1769480 | tf_op jit(solution)/shard_map/ppermute | solution.py:82
  312.4 7.1 %collective-permute-start.8 = (bf16[256,768]{1,0:T(8,128)(2,1)}, bf16[256,768]{1,0:T(8,128)(2,1)}, u32[]{:S(2)}, u32[]{:S(2)}) collective-permute-start(bf16[256,768]{1,0:T(8,128)(2,1)} %dynamic-slice_convert_fusion.2), channel_id=1, source_target_pairs={{0,1},{1,0},{2,3},{3,2},{4,5},{5,4},{6,7},{7,6},{8,9},{9,8},{10,11... | collective-permute-start | bytes 1179656 | tf_op jit(solution)/shard_map/ppermute | solution.py:63
  339.4 24.5 %collective-permute-start.9 = (bf16[256,768]{1,0:T(8,128)(2,1)}, bf16[256,768]{1,0:T(8,128)(2,1)S(1)}, u32[]{:S(2)}, u32[]{:S(2)}) collective-permute-start(bf16[256,768]{1,0:T(8,128)(2,1)} %dynamic-slice_convert_fusion.1), channel_id=1, source_target_pairs={{0,1},{1,0},{2,3},{3,2},{4,5},{5,4},{6,7},{7,6},{8,9},{9,8},{10,11... | collective-permute-start | bytes 1179656 | tf_op jit(solution)/shard_map/ppermute | solution.py:63
  353.0 81.8 %collective-permute-start.24 = (bf16[2,4,4,24,768]{4,3,1,2,0:T(8,128)(2,1)}, bf16[2,4,4,24,768]{4,3,1,2,0:T(8,128)(2,1)}, u32[]{:S(2)}, u32[]{:S(2)}) collective-permute-start(bf16[2,4,4,24,768]{4,3,1,2,0:T(8,128)(2,1)} %pad_maximum_fusion.24), channel_id=1, source_target_pairs={{0,8},{8,0},{16,24},{24,16},{1,9},{9,1},{17,25},{25,17},{2,10},{10... | collective-permute-start | bytes 3538952 | tf_op jit(solution)/shard_map/ppermute | solution.py:80
  356.2 82.8 %collective-permute-start.36 = (bf16[2,4,4,24,768]{4,3,2,1,0:T(8,128)(2,1)}, bf16[2,4,4,24,768]{4,3,2,1,0:T(8,128)(2,1)}, u32[]{:S(2)}, u32[]{:S(2)}) collective-permute-start(bf16[2,4,4,24,768]{4,3,2,1,0:T(8,128)(2,1)} %pad_maximum_fusion.26), channel_id=1, source_target_pairs={{0,32},{32,0},{64,96},{96,64},{1,33},{33,1},{65,97},{97,65},{2,34}... | collective-permute-start | bytes 3538952 | tf_op jit(solution)/shard_map/ppermute | solution.py:80
  358.9 40.3 %collective-permute-start.32 = (bf16[2,4,24,768]{3,2,1,0:T(8,128)(2,1)}, bf16[2,4,24,768]{3,2,1,0:T(8,128)(2,1)}, u32[]{:S(2)}, u32[]{:S(2)}) collective-permute-start(bf16[2,4,24,768]{3,2,1,0:T(8,128)(2,1)} %pad_maximum_fusion.41), channel_id=1, source_target_pairs={{0,6},{2,4},{4,2},{6,0},{1,7},{3,5},{5,3},{7,1},{8,14},{10,12},{12... | collective-permute-start | bytes 884744 | tf_op jit(solution)/shard_map/ppermute | solution.py:80
  363.5 38.1 %collective-permute-start.44 = (bf16[2,4,24,768]{3,2,1,0:T(8,128)(2,1)}, bf16[2,4,24,768]{3,2,1,0:T(8,128)(2,1)}, u32[]{:S(2)}, u32[]{:S(2)}) collective-permute-start(bf16[2,4,24,768]{3,2,1,0:T(8,128)(2,1)} %pad_maximum_fusion.43), channel_id=1, source_target_pairs={{0,8},{8,0},{16,24},{24,16},{1,9},{9,1},{17,25},{25,17},{2,10},{10... | collective-permute-start | bytes 884744 | tf_op jit(solution)/shard_map/ppermute | solution.py:80
  397.8 44.9 %collective-permute-start.10 = (bf16[512,768]{0,1:T(8,128)(2,1)}, bf16[512,768]{0,1:T(8,128)(2,1)S(1)}, u32[]{:S(2)}, u32[]{:S(2)}) collective-permute-start(bf16[512,768]{0,1:T(8,128)(2,1)} %fusion.59), channel_id=1, source_target_pairs={{0,2},{2,0},{1,3},{3,1},{4,6},{6,4},{5,7},{7,5},{8,10},{10,8},{9,1... | collective-permute-start | bytes 2359304 | tf_op jit(solution)/shard_map/ppermute | solution.py:67
  400.2 20.6 %collective-permute-start.33 = (bf16[4,24,768]{2,1,0:T(8,128)(2,1)S(1)}, bf16[4,24,768]{2,1,0:T(8,128)(2,1)S(1)}, u32[]{:S(2)}, u32[]{:S(2)}) collective-permute-start(bf16[4,24,768]{2,1,0:T(8,128)(2,1)S(1)} %fusion.132), channel_id=1, source_target_pairs={{0,2},{2,0},{4,6},{6,4},{1,3},{3,1},{5,7},{7,5},{8,10},{10,8},{12,... | collective-permute-start | bytes 442376 | tf_op jit(solution)/shard_map/ppermute | solution.py:82
  402.7 20.7 %collective-permute-start.45 = (bf16[4,24,768]{2,1,0:T(8,128)(2,1)S(1)}, bf16[4,24,768]{2,1,0:T(8,128)(2,1)S(1)}, u32[]{:S(2)}, u32[]{:S(2)}) collective-permute-start(bf16[4,24,768]{2,1,0:T(8,128)(2,1)S(1)} %fusion.149), channel_id=1, source_target_pairs={{0,24},{8,16},{16,8},{24,0},{1,25},{9,17},{17,9},{25,1},{2,26},{10... | collective-permute-start | bytes 442376 | tf_op jit(solution)/shard_map/ppermute | solution.py:82
  437.1 55.1 %collective-permute-start.25 = (bf16[4,4,24,768]{3,2,0,1:T(8,128)(2,1)}, bf16[4,4,24,768]{3,2,0,1:T(8,128)(2,1)}, u32[]{:S(2)}, u32[]{:S(2)}) collective-permute-start(bf16[4,4,24,768]{3,2,0,1:T(8,128)(2,1)} %fusion.78), channel_id=1, source_target_pairs={{0,24},{8,16},{16,8},{24,0},{1,25},{9,17},{17,9},{25,1},{2,26},{10... | collective-permute-start | bytes 1769480 | tf_op jit(solution)/shard_map/ppermute | solution.py:82
  441.2 54.3 %collective-permute-start.37 = (bf16[4,4,24,768]{3,2,1,0:T(8,128)(2,1)}, bf16[4,4,24,768]{3,2,1,0:T(8,128)(2,1)}, u32[]{:S(2)}, u32[]{:S(2)}) collective-permute-start(bf16[4,4,24,768]{3,2,1,0:T(8,128)(2,1)} %fusion.108), channel_id=1, source_target_pairs={{0,96},{32,64},{64,32},{96,0},{1,97},{33,65},{65,33},{97,1},{2,98}... | collective-permute-start | bytes 1769480 | tf_op jit(solution)/shard_map/ppermute | solution.py:82
  474.1 81.7 %collective-permute-start.18 = (bf16[2,4,4,24,896]{4,3,2,1,0:T(8,128)(2,1)}, bf16[2,4,4,24,896]{4,3,2,1,0:T(8,128)(2,1)}, u32[]{:S(2)}, u32[]{:S(2)}) collective-permute-start(bf16[2,4,4,24,896]{4,3,2,1,0:T(8,128)(2,1)} %pad_maximum_fusion.23), channel_id=1, source_target_pairs={{0,6},{2,4},{4,2},{6,0},{1,7},{3,5},{5,3},{7,1},{8,14},{10,12},{12... | collective-permute-start | bytes 4128776 | tf_op jit(solution)/shard_map/ppermute | solution.py:80
  490.1 68.8 %collective-permute-start.12 = (bf16[2,4,4,24,896]{4,3,2,1,0:T(8,128)(2,1)S(1)}, bf16[2,4,4,24,896]{4,3,2,1,0:T(8,128)(2,1)S(1)}, u32[]{:S(2)}, u32[]{:S(2)}) collective-permute-start(bf16[2,4,4,24,896]{4,3,2,1,0:T(8,128)(2,1)S(1)} %pad_maximum_fusion.22), channel_id=1, source_target_pairs={{0,6},{2,4},{4,2},{6,0},{1,7},{3,5},{5,3},{7,1},{8,14},{10,12},{12... | collective-permute-start | bytes 4128776 | tf_op jit(solution)/shard_map/ppermute | solution.py:80
  493.9 49.6 %collective-permute-start.26 = (bf16[2,4,24,768]{3,2,1,0:T(8,128)(2,1)S(1)}, bf16[2,4,24,768]{3,2,1,0:T(8,128)(2,1)S(1)}, u32[]{:S(2)}, u32[]{:S(2)}) collective-permute-start(bf16[2,4,24,768]{3,2,1,0:T(8,128)(2,1)S(1)} %pad_maximum_fusion.40), channel_id=1, source_target_pairs={{0,6},{2,4},{4,2},{6,0},{1,7},{3,5},{5,3},{7,1},{8,14},{10,12},{12... | collective-permute-start | bytes 884744 | tf_op jit(solution)/shard_map/ppermute | solution.py:80
  497.2 46.5 %collective-permute-start.38 = (bf16[2,4,24,768]{3,2,1,0:T(8,128)(2,1)S(1)}, bf16[2,4,24,768]{3,2,1,0:T(8,128)(2,1)S(1)}, u32[]{:S(2)}, u32[]{:S(2)}) collective-permute-start(bf16[2,4,24,768]{3,2,1,0:T(8,128)(2,1)S(1)} %pad_maximum_fusion.42), channel_id=1, source_target_pairs={{0,8},{8,0},{16,24},{24,16},{1,9},{9,1},{17,25},{25,17},{2,10},{10... | collective-permute-start | bytes 884744 | tf_op jit(solution)/shard_map/ppermute | solution.py:80
  557.0 18.5 %collective-permute-start.19 = (bf16[4,4,24,896]{3,2,1,0:T(8,128)(2,1)S(1)}, bf16[4,4,24,896]{3,2,1,0:T(8,128)(2,1)S(1)}, u32[]{:S(2)}, u32[]{:S(2)}) collective-permute-start(bf16[4,4,24,896]{3,2,1,0:T(8,128)(2,1)S(1)} %fusion.65), channel_id=1, source_target_pairs={{0,2},{2,0},{4,6},{6,4},{1,3},{3,1},{5,7},{7,5},{8,10},{10,8},{12,... | collective-permute-start | bytes 2064392 | tf_op jit(solution)/shard_map/ppermute | solution.py:82
  559.1 27.4 %collective-permute-start.13 = (bf16[4,4,24,896]{3,2,1,0:T(8,128)(2,1)S(1)}, bf16[4,4,24,896]{3,2,1,0:T(8,128)(2,1)S(1)}, u32[]{:S(2)}, u32[]{:S(2)}) collective-permute-start(bf16[4,4,24,896]{3,2,1,0:T(8,128)(2,1)S(1)} %fusion.68), channel_id=1, source_target_pairs={{0,2},{2,0},{4,6},{6,4},{1,3},{3,1},{5,7},{7,5},{8,10},{10,8},{12,... | collective-permute-start | bytes 2064392 | tf_op jit(solution)/shard_map/ppermute | solution.py:82
  577.0 11.7 %collective-permute-start.20 = (bf16[2,4,24,896]{3,2,1,0:T(8,128)(2,1)S(1)}, bf16[2,4,24,896]{3,2,1,0:T(8,128)(2,1)S(1)}, u32[]{:S(2)}, u32[]{:S(2)}) collective-permute-start(bf16[2,4,24,896]{3,2,1,0:T(8,128)(2,1)S(1)} %pad_maximum_fusion.39), channel_id=1, source_target_pairs={{0,32},{32,0},{64,96},{96,64},{1,33},{33,1},{65,97},{97,65},{2,34}... | collective-permute-start | bytes 1032200 | tf_op jit(solution)/shard_map/ppermute | solution.py:80
  586.9 7.3 %collective-permute-start.14 = (bf16[2,4,24,896]{3,2,1,0:T(8,128)(2,1)S(1)}, bf16[2,4,24,896]{3,2,1,0:T(8,128)(2,1)S(1)}, u32[]{:S(2)}, u32[]{:S(2)}) collective-permute-start(bf16[2,4,24,896]{3,2,1,0:T(8,128)(2,1)S(1)} %pad_maximum_fusion.38), channel_id=1, source_target_pairs={{0,32},{32,0},{64,96},{96,64},{1,33},{33,1},{65,97},{97,65},{2,34}... | collective-permute-start | bytes 1032200 | tf_op jit(solution)/shard_map/ppermute | solution.py:80
  588.7 8.5 %collective-permute-start.21 = (bf16[4,24,896]{2,1,0:T(8,128)(2,1)S(1)}, bf16[4,24,896]{2,1,0:T(8,128)(2,1)S(1)}, u32[]{:S(2)}, u32[]{:S(2)}) collective-permute-start(bf16[4,24,896]{2,1,0:T(8,128)(2,1)S(1)} %fusion.147), channel_id=1, source_target_pairs={{0,96},{32,64},{64,32},{96,0},{1,97},{33,65},{65,33},{97,1},{2,98}... | collective-permute-start | bytes 516104 | tf_op jit(solution)/shard_map/ppermute | solution.py:82
  (169 other events, 1056.7 us)
Sparse Core Ops, SparseCore 0:
  15.7 77.7 all-gather.4
  96.8 74.1 all-gather.6
